TPU v7x, 32 devices: a whole 2x2x4 slice. The times are simulated.
32 devices in a mesh: dp: 4 (over x, core), expert: 8 (over z, y).
Axes of the slice: x: 2, y: 2, z: 4, core: 2. Of those that a mesh axis runs over, the one named last changes fastest.
Arguments:
- tokens: bfloat16 [1024, 3584], P('expert', 'dp'), may hold values from -6 to 6
- routes: int32 [1024, 4], P('expert'), may hold values from 0 to 7, all different within a row; in each aligned block of 128 rows (0 to 127, 128 to 255, ...) at most 96 rows name the same one
- gates: float32 [1024, 4], P('expert'), may hold values from 0.1 to 1
- w_gate: bfloat16 [8, 3584, 1024], P('expert', 'dp'), may hold values from -0.09375 to 0.09375
- w_up: bfloat16 [8, 3584, 1024], P('expert', 'dp'), may hold values from -0.09375 to 0.09375
- w_down: bfloat16 [8, 1024, 3584], P('expert', None, 'dp'), may hold values from -0.1875 to 0.1875
- cotangent: bfloat16 [1024, 3584], P('expert', 'dp'), may hold values from -1.5 to 1.5
Outputs:
- mixed: bfloat16 [1024, 3584], P('expert', 'dp')
- token_grad: bfloat16 [1024, 3584], P('expert', 'dp')
- gate_grad: float32 [1024, 4], P('expert')
- w_gate_grad: bfloat16 [8, 3584, 1024], P('expert', 'dp')
- w_up_grad: bfloat16 [8, 3584, 1024], P('expert', 'dp')
- w_down_grad: bfloat16 [8, 1024, 3584], P('expert', None, 'dp')
Inputs may be any that keep to these rules, and one draw needn't show every extreme that they name: `routes`: each row names 4 different experts. Within the 128 rows of one index of the expert axis (aligned blocks of rows), no expert is named more than 96 times, and in every draw some expert is named exactly 96 times in some block.
All inputs are finite; a program needn't handle non-finite values.
Results may differ from a plain program's by a relative error of at most 0.028.
Values may be sent and summed in bfloat16 or wider, within the bound.
A program may use at most 128 MiB of HBM per device.

v0:
```python
import functools

import jax
import jax.numpy as jnp
from jax import lax
from jax.experimental import pallas as pl
from jax.experimental.pallas import tpu as pltpu
from jax.sharding import PartitionSpec as P

BF = jnp.bfloat16
F32 = jnp.float32


def dot(a, b):
    return jnp.dot(a, b, preferred_element_type=F32)


def dot_t(a, b):
    return lax.dot_general(a, b, (((0,), (0,)), ((), ())), preferred_element_type=F32)


def dot_nt(a, b):
    return lax.dot_general(a, b, (((1,), (1,)), ((), ())), preferred_element_type=F32)


def hop(v, bit):
    count = lax.axis_size("dp")
    return lax.ppermute(v, "dp", [(i, i ^ bit) for i in range(count)])


def reduce_rows(p):
    q = p.shape[0] // 4
    sent = jnp.concatenate([p[q:2 * q], p[3 * q:]], axis=0)
    got = hop(sent, 1)
    kept = p[:q].astype(F32) + got[:q].astype(F32)
    other = (p[2 * q:3 * q].astype(F32) + got[q:].astype(F32)).astype(BF)
    return kept + hop(other, 2).astype(F32)


def gather_rows(h):
    both = jnp.concatenate([h, hop(h, 2)], axis=0)
    far = hop(both, 1)
    q = h.shape[0]
    return jnp.concatenate([both[:q], far[:q], both[q:], far[q:]], axis=0)


MESH = pl.DeviceIdType.MESH
VM = pl.BlockSpec(memory_space=pltpu.VMEM)


def greet(z, y, lines):
    barrier = pltpu.get_barrier_semaphore()
    me = z * 2 + y

    def call(dev):
        pl.semaphore_signal(barrier, inc=1, device_id={"expert": dev}, device_id_type=MESH)

    call(me + 1 - 2 * y)
    pl.when(z > 0)(lambda: call(me - 2))
    pl.when(z < lines - 1)(lambda: call(me + 2))
    peers = 1 + jnp.where(z > 0, 1, 0) + jnp.where(z < lines - 1, 1, 0)
    pl.semaphore_wait(barrier, peers)


def gather_kernel(lines, *refs):
    n = 3
    own, full = refs[:n], refs[n:2 * n]
    ssem, rsem, lsem = refs[2 * n:]
    me = lax.axis_index("expert")
    z, y = me // 2, me % 2
    partner = me + 1 - 2 * y

    def move(a, way, owner, dev, src=None):
        return pltpu.make_async_remote_copy(
            src_ref=full[a].at[owner] if src is None else src,
            dst_ref=full[a].at[owner],
            send_sem=ssem.at[a, way, owner],
            recv_sem=rsem.at[a, owner],
            device_id={"expert": dev},
            device_id_type=MESH,
        )

    greet(z, y, lines)
    for a in range(n):
        pl.when(z < lines - 1)(lambda: move(a, 0, me, me + 2, own[a]).start())
        pl.when(z > 0)(lambda: move(a, 1, me, me - 2, own[a]).start())
        move(a, 2, me, partner, own[a]).start()
    local = [pltpu.make_async_copy(own[a], full[a].at[me], lsem.at[a]) for a in range(n)]
    for copy in local:
        copy.start()
    for a in range(n):
        for s in range(1, lines):
            @pl.when(z >= s)
            def _():
                owner = me - 2 * s
                move(a, 0, owner, partner).wait_recv()
                pl.when(z < lines - 1)(lambda: move(a, 0, owner, me + 2).start())
                move(a, 2, owner, partner).start()

            @pl.when(z + s < lines)
            def _():
                owner = me + 2 * s
                move(a, 1, owner, partner).wait_recv()
                pl.when(z > 0)(lambda: move(a, 1, owner, me - 2).start())
                move(a, 2, owner, partner).start()
    for a in range(n):
        for line in range(lines):
            move(a, 2, line * 2 + 1 - y, partner).wait_recv()
            move(a, 2, line * 2 + y, partner).wait_send()

            @pl.when((line <= z) & (z < lines - 1))
            def _():
                move(a, 0, line * 2 + y, partner).wait_send()

            @pl.when((line >= z) & (z > 0))
            def _():
                move(a, 1, line * 2 + y, partner).wait_send()
    for copy in local:
        copy.wait()


def all_rows(experts, *blocks):
    n = len(blocks)
    return pl.pallas_call(
        functools.partial(gather_kernel, experts // 2),
        out_shape=[jax.ShapeDtypeStruct((experts,) + b.shape, b.dtype) for b in blocks],
        in_specs=[VM] * n,
        out_specs=[VM] * n,
        scratch_shapes=[
            pltpu.SemaphoreType.DMA((n, 3, experts)),
            pltpu.SemaphoreType.DMA((n, experts)),
            pltpu.SemaphoreType.DMA((n,)),
        ],
        compiler_params=pltpu.CompilerParams(
            collective_id=0, has_side_effects=True, vmem_limit_bytes=40 << 20
        ),
    )(*blocks)


def scatter_kernel(lines, *refs):
    n = 3
    full, out = refs[:n], refs[n:2 * n]
    ybuf, ubuf, dbuf, sbuf = (refs[(2 + i) * n:(3 + i) * n] for i in range(4))
    ysend, yrecv, zsend, urecv, drecv = refs[6 * n:]
    me = lax.axis_index("expert")
    z, y = me // 2, me % 2
    partner = me + 1 - 2 * y

    def across(a, line):
        return pltpu.make_async_remote_copy(
            src_ref=full[a].at[line * 2 + 1 - y],
            dst_ref=ybuf[a].at[line],
            send_sem=ysend.at[a, line],
            recv_sem=yrecv.at[a, line],
            device_id={"expert": partner},
            device_id_type=MESH,
        )

    def along(a, line, up):
        return pltpu.make_async_remote_copy(
            src_ref=sbuf[a].at[line],
            dst_ref=(ubuf if up else dbuf)[a].at[line],
            send_sem=zsend.at[a, line],
            recv_sem=(urecv if up else drecv).at[a, line],
            device_id={"expert": me + 2 if up else me - 2},
            device_id_type=MESH,
        )

    def base(a, line):
        across(a, line).wait_recv()
        return full[a][line * 2 + y].astype(F32) + ybuf[a][line].astype(F32)

    greet(z, y, lines)
    for a in range(n):
        for s in range(lines - 1, 0, -1):
            pl.when(z + s < lines)(lambda: across(a, z + s).start())
            pl.when(z >= s)(lambda: across(a, z - s).start())
        across(a, z).start()
    for a in range(n):
        for s in range(lines - 1, 0, -1):
            @pl.when(z + s < lines)
            def _():
                line = z + s
                sbuf[a][line] = base(a, line).astype(sbuf[a].dtype)

                @pl.when(z > 0)
                def _():
                    along(a, line, True).wait_recv()
                    sbuf[a][line] = (
                        sbuf[a][line].astype(F32) + ubuf[a][line].astype(F32)
                    ).astype(sbuf[a].dtype)

                along(a, line, True).start()

            @pl.when(z >= s)
            def _():
                line = z - s
                sbuf[a][line] = base(a, line).astype(sbuf[a].dtype)

                @pl.when(z < lines - 1)
                def _():
                    along(a, line, False).wait_recv()
                    sbuf[a][line] = (
                        sbuf[a][line].astype(F32) + dbuf[a][line].astype(F32)
                    ).astype(sbuf[a].dtype)

                along(a, line, False).start()
    for a in range(n):
        pl.when(z > 0)(lambda: along(a, z, True).wait_recv())
        pl.when(z < lines - 1)(lambda: along(a, z, False).wait_recv())
        total = base(a, z)
        total = total + jnp.where(z > 0, ubuf[a][z].astype(F32), 0.0)
        total = total + jnp.where(z < lines - 1, dbuf[a][z].astype(F32), 0.0)
        out[a][...] = total.astype(out[a].dtype)
        for line in range(lines):
            across(a, line).wait_send()
            pl.when(z != line)(lambda: along(a, line, True).wait_send())


def sum_rows(experts, *blocks):
    n, lines = len(blocks), experts // 2
    half = [pltpu.VMEM((lines,) + b.shape[1:], b.dtype) for b in blocks]
    return pl.pallas_call(
        functools.partial(scatter_kernel, lines),
        out_shape=[jax.ShapeDtypeStruct(b.shape[1:], b.dtype) for b in blocks],
        in_specs=[VM] * n,
        out_specs=[VM] * n,
        scratch_shapes=half * 4 + [pltpu.SemaphoreType.DMA((n, lines))] * 5,
        compiler_params=pltpu.CompilerParams(
            collective_id=1, has_side_effects=True, vmem_limit_bytes=40 << 20
        ),
    )(*blocks)


def per_device(tokens, routes, gates, w_gate, w_up, w_down, cotangent):
    tok_rows, quarter = tokens.shape
    top_count = routes.shape[1]
    experts = lax.axis_size("expert")
    capacity = max(2, (3 * tok_rows * top_count + 2 * experts - 1) // (2 * experts))
    slots = experts * capacity
    q = slots // 4
    me = lax.axis_index("expert")
    d = lax.axis_index("dp")
    wg, wu, wd = w_gate[0], w_up[0], w_down[0]

    labels = jnp.arange(experts, dtype=jnp.int32)
    chosen = routes[:, :, None] == labels[None, None, :]
    table = jnp.sum(jnp.where(chosen, gates[:, :, None], 0.0), axis=1)
    near = experts == 8
    if near:
        tables, x, c = all_rows(experts, table.T, tokens, cotangent)
        weight = lax.dynamic_index_in_dim(tables, me, axis=1, keepdims=False)
        x = x.reshape(experts * tok_rows, quarter)
        c = c.reshape(experts * tok_rows, quarter)
    else:
        weight = lax.all_to_all(table.T, "expert", split_axis=0, concat_axis=0, tiled=True)
        x = lax.all_gather(tokens, "expert", axis=0, tiled=True)
        c = lax.all_gather(cotangent, "expert", axis=0, tiled=True)
    weight = weight.reshape(experts * tok_rows)

    routed = weight > 0.0
    rank = jnp.cumsum(routed.astype(jnp.int32)) - 1
    rank = jnp.where(routed, rank, -1)
    place = jnp.arange(slots, dtype=jnp.int32)
    place = (place // q ^ d) * q + place % q
    hit = place[:, None] == rank[None, :]
    pick = hit.astype(BF)
    slot_gate = jnp.sum(jnp.where(hit, weight[None, :], 0.0), axis=1)

    xs = dot(pick, x).astype(BF)
    gate_pre = reduce_rows(dot(xs, wg).astype(BF))
    up_pre = reduce_rows(dot(xs, wu).astype(BF))
    cs = dot(pick, c).astype(BF)
    raw_grad = reduce_rows(dot_nt(cs, wd).astype(BF))

    own_gate = slot_gate[:q, None]
    sig = jax.nn.sigmoid(gate_pre)
    active = gate_pre * sig
    hidden32 = active * up_pre
    hidden = gather_rows(hidden32.astype(BF))
    gate_inner = jnp.sum(hidden32 * raw_grad, axis=1)
    hidden_grad = raw_grad * own_gate
    gpg = gather_rows((hidden_grad * up_pre * sig * (1.0 + gate_pre * (1.0 - sig))).astype(BF))
    upg = gather_rows((hidden_grad * active).astype(BF))

    out = (dot(hidden, wd) * slot_gate[:, None]).astype(BF)
    out = dot_t(pick, out).astype(BF)
    pair = (dot_nt(gpg, wg) + dot_nt(upg, wu)).astype(BF)
    pair = dot_t(pick, pair).astype(BF)

    inner = gather_rows(gate_inner[:, None])
    inner = jnp.sum(jnp.where(hit, inner, 0.0), axis=0).reshape(experts, tok_rows)
    if near:
        mine = (labels == me)[None, :, None]
        inner, mixed, token_grad = sum_rows(
            experts,
            jnp.where(mine, inner[:, None, :], 0.0),
            out.reshape(experts, tok_rows, quarter),
            pair.reshape(experts, tok_rows, quarter),
        )
    else:
        inner = lax.all_to_all(inner, "expert", split_axis=0, concat_axis=0, tiled=True)
        mixed = lax.psum_scatter(out, "expert", scatter_dimension=0, tiled=True)
        token_grad = lax.psum_scatter(pair, "expert", scatter_dimension=0, tiled=True)
    gate_grad = jnp.sum(jnp.where(chosen, inner.T[:, None, :], 0.0), axis=2)

    w_down_grad = dot_t((hidden.astype(F32) * slot_gate[:, None]).astype(BF), cs).astype(BF)[None]
    w_gate_grad = dot_t(xs, gpg).astype(BF)[None]
    w_up_grad = dot_t(xs, upg).astype(BF)[None]
    return mixed, token_grad, gate_grad, w_gate_grad, w_up_grad, w_down_grad


def solution(mesh):
    placed = (
        P("expert", "dp"),
        P("expert", None),
        P("expert", None),
        P("expert", "dp", None),
        P("expert", "dp", None),
        P("expert", None, "dp"),
        P("expert", "dp"),
    )
    return jax.shard_map(
        per_device,
        mesh=mesh,
        in_specs=placed,
        out_specs=(
            P("expert", "dp"),
            P("expert", "dp"),
            P("expert", None),
            P("expert", "dp", None),
            P("expert", "dp", None),
            P("expert", None, "dp"),
        ),
        check_vma=False,
    )
```

profile of v0, /device:TPU:0, one launch (start us, length us, event | category | flops | bytes accessed | tf_op | source)
XLA Modules:
  0.0 212.6 jit_solution(15740132952050379509)
XLA Ops:
  0.7 0.8 select_reduce_fusion.1
  1.5 0.9 copy-done.3
  2.4 0.9 copy-done.4
  3.4 49.3 %shard_map.118 = (f32[8,8,128]{2,1,0:T(8,128)S(1)}, bf16[8,128,896]{2,1,0:T(8,128)(2,1)S(1)}, bf16[8,128,896]{2,1,0:T(8,128)(2,1)S(1)}) custom-call(f32[8,128]{1,0:T(8,128)S(1)} %bitcast.57, bf16[128,896]{1,0:T(8,128)(2,1)S(1)} %copy-done.3, bf16[128,896]{1,0:T(8,128)(2,1)S(1)} %copy-done.4), custom_call_target="tpu_custom_call" | custom-call | tf_op jit(solution)/shard_map/pallas_call | solution.py:124
  52.7 1.2 copy-done.5
  53.9 1.2 copy-done.7
  55.1 0.3 reduce-window.9
  55.7 3.5 %fusion.39 = bf16[768,896]{1,0:T(8,128)(2,1)S(1)} fusion(bf16[1024,896]{1,0:T(8,128)(2,1)} %bitcast.60, s32[1024]{0:T(1024)S(1)} %bitcast_select_fusion, s32[768]{0:T(1024)S(1)} %fusion.70), kind=kOutput, calls=%fused_computation.35 | convolution fusion | flops 1410760704 | bytes 3218432 | tf_op jit(solution)/shard_map/dot_general | solution.py:15
  59.2 1.8 fusion.28
  61.2 1.3 copy-done.21
  62.5 1.8 fusion.31
  64.5 1.3 copy-done.6
  65.8 1.8 fusion.42
  67.7 1.8 fusion.34
  69.9 1.6 collective-permute-start.1
  71.6 0.6 collective-permute-start.3
  72.3 1.6 collective-permute-start.5
  73.9 8.0 %collective-permute-done.1 = bf16[192,1024]{1,0:T(8,128)(2,1)S(1)} collective-permute-done((bf16[192,1024]{1,0:T(8,128)(2,1)S(1)}, bf16[192,1024]{1,0:T(8,128)(2,1)S(1)}, u32[]{:S(2)}, u32[]{:S(2)}) %collective-permute-start.1) | collective-permute-done | bytes 393248 | tf_op jit(solution)/shard_map/ppermute | solution.py:28
  81.9 8.4 %collective-permute-done.3 = bf16[192,1024]{1,0:T(8,128)(2,1)S(1)} collective-permute-done((bf16[192,1024]{1,0:T(8,128)(2,1)S(1)}, bf16[192,1024]{1,0:T(8,128)(2,1)S(1)}, u32[]{:S(2)}, u32[]{:S(2)}) %collective-permute-start.3) | collective-permute-done | bytes 393248 | tf_op jit(solution)/shard_map/ppermute | solution.py:28
  90.3 8.0 %collective-permute-done.5 = bf16[192,1024]{1,0:T(8,128)(2,1)S(1)} collective-permute-done((bf16[192,1024]{1,0:T(8,128)(2,1)S(1)}, bf16[192,1024]{1,0:T(8,128)(2,1)S(1)}, u32[]{:S(2)}, u32[]{:S(2)}) %collective-permute-start.5) | collective-permute-done | bytes 393248 | tf_op jit(solution)/shard_map/ppermute | solution.py:28
  98.3 0.7 multiply_reduce_fusion
  99.0 1.5 collective-permute-start.6
  100.5 2.1 collective-permute-done.6
  102.7 1.1 collective-permute-done.7
  104.0 0.7 fusion.9
  104.7 1.0 multiply_convert_fusion.4
  105.7 1.6 collective-permute-start.8
  107.3 0.5 collective-permute-start.12
  107.8 1.5 collective-permute-start.10
  109.3 8.4 %collective-permute-done.8 = bf16[192,1024]{1,0:T(8,128)(2,1)S(1)} collective-permute-done((bf16[192,1024]{1,0:T(8,128)(2,1)S(1)}, bf16[192,1024]{1,0:T(8,128)(2,1)S(1)}, u32[]{:S(2)}, u32[]{:S(2)}) %collective-permute-start.8) | collective-permute-done | bytes 393248 | tf_op jit(solution)/shard_map/ppermute | solution.py:28
  117.7 0.8 copy-done.10
  118.6 7.5 %collective-permute-done.12 = bf16[192,1024]{1,0:T(8,128)(2,1)S(1)} collective-permute-done((bf16[192,1024]{1,0:T(8,128)(2,1)S(1)}, bf16[192,1024]{1,0:T(8,128)(2,1)S(1)}, u32[]{:S(2)}, u32[]{:S(2)}) %collective-permute-start.12) | collective-permute-done | bytes 393248 | tf_op jit(solution)/shard_map/ppermute | solution.py:28
  126.3 7.5 %collective-permute-done.10 = bf16[192,1024]{1,0:T(8,128)(2,1)S(1)} collective-permute-done((bf16[192,1024]{1,0:T(8,128)(2,1)S(1)}, bf16[192,1024]{1,0:T(8,128)(2,1)S(1)}, u32[]{:S(2)}, u32[]{:S(2)}) %collective-permute-start.10) | collective-permute-done | bytes 393248 | tf_op jit(solution)/shard_map/ppermute | solution.py:28
  134.0 0.9 fusion.86
  135.1 1.2 collective-permute-done.11
  136.2 1.0 fusion.84
  137.2 3.5 %fusion.14 = f32[768,896]{1,0:T(8,128)} fusion(bf16[1,896,1024]{2,1,0:T(8,128)(2,1)S(1)} %copy-done.21, bf16[192,1024]{1,0:T(8,128)(2,1)S(1)} %get-tuple-element.34, bf16[192,1024]{1,0:T(8,128)(2,1)S(1)} %collective-permute-done.12, bf16[192,1024]{1,0:T(8,128)(2,1)S(1)} %get-tuple-element.33, bf16[192,1024]{1,0:T(8,128)(2,1)S(1)} %get-tuple-element.23), kind=kOutput, calls=%fused_computation.19 | convolution fusion | flops 1415577600 | bytes 6160384 | tf_op jit(solution)/shard_map/dot_general | solution.py:23
  140.7 5.9 %fusion.22 = bf16[1024,896]{1,0:T(8,128)(2,1)} fusion(s32[1024]{0:T(1024)S(1)} %bitcast_select_fusion, s32[768]{0:T(1024)S(1)} %fusion.70, bf16[1,1024,896]{2,1,0:T(8,128)(2,1)S(1)} %copy-done, f32[768]{0:T(1024)S(1)} %get-tuple-element.18, bf16[192,1024]{1,0:T(8,128)(2,1)} %get-tuple-element.36, bf16[192,1024]{1,0:T(8,128)(2,1)} %copy-done.10, ...), kind=kOutput, calls=%fused_computation.30 | convolution fusion | flops 2827943936 | bytes 5253120 | tf_op jit(solution)/shard_map/dot_general | solution.py:19
  146.6 7.3 %fusion.25 = bf16[1024,896]{1,0:T(8,128)(2,1)} fusion(s32[1024]{0:T(1024)S(1)} %bitcast_select_fusion, s32[768]{0:T(1024)S(1)} %fusion.70, f32[768,896]{1,0:T(8,128)} %fusion.14, bf16[1,896,1024]{2,1,0:T(8,128)(2,1)} %param.10, bf16[192,1024]{1,0:T(8,128)(2,1)} %get-tuple-element.32, bf16[192,1024]{1,0:T(8,128)(2,1)S(1)} %collective-permute-done.10, ...), kind=kOutput, calls=%fused_computation.31 | convolution fusion | flops 2827943936 | bytes 8002560 | tf_op jit(solution)/shard_map/dot_general | solution.py:19
  153.9 1.5 copy-done.1
  155.4 1.5 copy-done.2
  156.9 44.7 %shard_map.119 = (f32[8,128]{1,0:T(8,128)S(1)}, bf16[128,896]{1,0:T(8,128)(2,1)S(1)}, bf16[128,896]{1,0:T(8,128)(2,1)S(1)}) custom-call(f32[8,8,128]{2,1,0:T(8,128)S(1)} %broadcast_select_fusion.refs_0_, bf16[8,128,896]{2,1,0:T(8,128)(2,1)S(1)} %bitcast.55, bf16[8,128,896]{2,1,0:T(8,128)(2,1)S(1)} %bitcast.56), custom_call_target="tpu_custom_call" | custom-call | tf_op jit(solution)/shard_map/pallas_call | solution.py:223
  201.6 0.6 select_reduce_fusion
  202.2 3.2 %convert_bitcast_fusion = bf16[1,1024,896]{2,1,0:T(8,128)(2,1)} fusion(bf16[768,896]{1,0:T(8,128)(2,1)S(1)} %copy-done.26, f32[768]{0:T(1024)S(1)} %get-tuple-element.18, bf16[192,1024]{1,0:T(8,128)(2,1)S(1)} %copy-done.13, bf16[192,1024]{1,0:T(8,128)(2,1)S(1)} %copy-done.11, bf16[192,1024]{1,0:T(8,128)(2,1)S(1)} %copy-done.12, ...), kind=kOutput, calls=%fused_computation.27 | convolution fusion | flops 1418067968 | bytes 4787200 | tf_op jit(solution)/shard_map/dot_general | solution.py:19
  205.5 2.9 %convert_bitcast_fusion.1 = bf16[1,896,1024]{2,1,0:T(8,128)(2,1)} fusion(bf16[768,896]{1,0:T(8,128)(2,1)S(1)} %copy-done.24, bf16[192,1024]{1,0:T(8,128)(2,1)S(1)} %copy-done.17, bf16[192,1024]{1,0:T(8,128)(2,1)S(1)} %copy-done.9, bf16[192,1024]{1,0:T(8,128)(2,1)S(1)} %copy-done.15, bf16[192,1024]{1,0:T(8,128)(2,1)S(1)} %get-tuple-element.23), kind=kOutput, calls=%fused_computation.28 | convolution fusion | flops 1416495104 | bytes 4784128 | tf_op jit(solution)/shard_map/dot_general | solution.py:19
  208.4 2.9 %convert_bitcast_fusion.2 = bf16[1,896,1024]{2,1,0:T(8,128)(2,1)} fusion(bf16[768,896]{1,0:T(8,128)(2,1)S(1)} %copy-done.24, bf16[192,1024]{1,0:T(8,128)(2,1)S(1)} %copy-done.19, bf16[192,1024]{1,0:T(8,128)(2,1)S(1)} %collective-permute-done.10, bf16[192,1024]{1,0:T(8,128)(2,1)S(1)} %copy-done.18, bf16[192,1024]{1,0:T(8,128)(2,1)S(1)} %get-tuple-element.22), kind=kOutput, calls=%fused_computation.29 | convolution fusion | flops 1416495104 | bytes 4784128 | tf_op jit(solution)/shard_map/dot_general | solution.py:19
  211.2 0.7 copy.21
  211.9 0.7 copy.22
  (82 shorter events, 2.1 us)
Async XLA Ops:
  0.6 67.0 %copy-start = (bf16[1,1024,896]{2,1,0:T(8,128)(2,1)S(1)}, bf16[1,1024,896]{2,1,0:T(8,128)(2,1)}, u32[]{:S(2)}) copy-start(bf16[1,1024,896]{2,1,0:T(8,128)(2,1)} %param.12) | copy-start | bytes 5505028
  1.5 0.9 copy-start.3
  2.4 0.9 copy-start.4
  52.7 1.2 copy-start.5
  53.9 1.2 copy-start.7
  55.7 3.5 %copy-start.22 = (bf16[1,896,1024]{2,1,0:T(8,128)(2,1)S(1)}, bf16[1,896,1024]{2,1,0:T(8,128)(2,1)}, u32[]{:S(2)}) copy-start(bf16[1,896,1024]{2,1,0:T(8,128)(2,1)} %param.10) | copy-start | bytes 5505028
  59.2 2.0 copy-start.23
  61.0 1.5 copy-start.21
  61.2 8.6 %collective-permute-start = (bf16[384,1024]{1,0:T(8,128)(2,1)S(1)}, bf16[384,1024]{1,0:T(8,128)(2,1)S(1)}, u32[]{:S(2)}, u32[]{:S(2)}) collective-permute-start(bf16[384,1024]{1,0:T(8,128)(2,1)S(1)} %pad_maximum_fusion.3), channel_id=1, source_target_pairs={{0,8},{8,0},{16,24},{24,16},{1,9},{9,1},{17,25},{25,17},{2,10},{10... | collective-permute-start | bytes 2359304 | tf_op jit(solution)/shard_map/ppermute | solution.py:28
  64.3 1.5 copy-start.6
  64.5 7.0 %collective-permute-start.2 = (bf16[384,1024]{1,0:T(8,128)(2,1)S(1)}, bf16[384,1024]{1,0:T(8,128)(2,1)S(1)}, u32[]{:S(2)}, u32[]{:S(2)}) collective-permute-start(bf16[384,1024]{1,0:T(8,128)(2,1)S(1)} %pad_maximum_fusion.4), channel_id=1, source_target_pairs={{0,8},{8,0},{16,24},{24,16},{1,9},{9,1},{17,25},{25,17},{2,10},{10... | collective-permute-start | bytes 2359304 | tf_op jit(solution)/shard_map/ppermute | solution.py:28
  67.7 1.9 copy-start.25
  69.7 2.5 %collective-permute-start.4 = (bf16[384,1024]{1,0:T(8,128)(2,1)S(1)}, bf16[384,1024]{1,0:T(8,128)(2,1)S(1)}, u32[]{:S(2)}, u32[]{:S(2)}) collective-permute-start(bf16[384,1024]{1,0:T(8,128)(2,1)S(1)} %pad_maximum_fusion.5), channel_id=1, source_target_pairs={{0,8},{8,0},{16,24},{24,16},{1,9},{9,1},{17,25},{25,17},{2,10},{10... | collective-permute-start | bytes 2359304 | tf_op jit(solution)/shard_map/ppermute | solution.py:28
  69.9 12.0 %collective-permute-start.1 = (bf16[192,1024]{1,0:T(8,128)(2,1)S(1)}, bf16[192,1024]{1,0:T(8,128)(2,1)S(1)}, u32[]{:S(2)}, u32[]{:S(2)}) collective-permute-start(bf16[192,1024]{1,0:T(8,128)(2,1)S(1)} %add_convert_fusion.3), channel_id=1, source_target_pairs={{0,16},{8,24},{16,0},{24,8},{1,17},{9,25},{17,1},{25,9},{2,18},{10... | collective-permute-start | bytes 1179656 | tf_op jit(solution)/shard_map/ppermute | solution.py:28
  71.6 18.7 %collective-permute-start.3 = (bf16[192,1024]{1,0:T(8,128)(2,1)S(1)}, bf16[192,1024]{1,0:T(8,128)(2,1)S(1)}, u32[]{:S(2)}, u32[]{:S(2)}) collective-permute-start(bf16[192,1024]{1,0:T(8,128)(2,1)S(1)} %add_convert_fusion.2), channel_id=1, source_target_pairs={{0,16},{8,24},{16,0},{24,8},{1,17},{9,25},{17,1},{25,9},{2,18},{10... | collective-permute-start | bytes 1179656 | tf_op jit(solution)/shard_map/ppermute | solution.py:28
  72.3 26.0 %collective-permute-start.5 = (bf16[192,1024]{1,0:T(8,128)(2,1)S(1)}, bf16[192,1024]{1,0:T(8,128)(2,1)S(1)}, u32[]{:S(2)}, u32[]{:S(2)}) collective-permute-start(bf16[192,1024]{1,0:T(8,128)(2,1)S(1)} %add_convert_fusion.1), channel_id=1, source_target_pairs={{0,16},{8,24},{16,0},{24,8},{1,17},{9,25},{17,1},{25,9},{2,18},{10... | collective-permute-start | bytes 1179656 | tf_op jit(solution)/shard_map/ppermute | solution.py:28
  99.0 3.6 %collective-permute-start.6 = (f32[192,1]{0,1:T(1,128)S(1)}, f32[192,1]{0,1:T(1,128)S(1)}, u32[]{:S(2)}, u32[]{:S(2)}) collective-permute-start(f32[192,1]{0,1:T(1,128)S(1)} %bitcast.65), channel_id=1, source_target_pairs={{0,16},{8,24},{16,0},{24,8},{1,17},{9,25},{17,1},{25,9},{2,18},{10... | collective-permute-start | bytes 2312 | tf_op jit(solution)/shard_map/ppermute | solution.py:28
  102.7 1.2 collective-permute-start.7
  105.7 12.0 %collective-permute-start.8 = (bf16[192,1024]{1,0:T(8,128)(2,1)S(1)}, bf16[192,1024]{1,0:T(8,128)(2,1)S(1)}, u32[]{:S(2)}, u32[]{:S(2)}) collective-permute-start(bf16[192,1024]{1,0:T(8,128)(2,1)S(1)} %get-tuple-element.24), channel_id=1, source_target_pairs={{0,16},{8,24},{16,0},{24,8},{1,17},{9,25},{17,1},{25,9},{2,18},{10... | collective-permute-start | bytes 1179656 | tf_op jit(solution)/shard_map/ppermute | solution.py:28
  107.3 18.9 %collective-permute-start.12 = (bf16[192,1024]{1,0:T(8,128)(2,1)S(1)}, bf16[192,1024]{1,0:T(8,128)(2,1)S(1)}, u32[]{:S(2)}, u32[]{:S(2)}) collective-permute-start(bf16[192,1024]{1,0:T(8,128)(2,1)S(1)} %get-tuple-element.23), channel_id=1, source_target_pairs={{0,16},{8,24},{16,0},{24,8},{1,17},{9,25},{17,1},{25,9},{2,18},{10... | collective-permute-start | bytes 1179656 | tf_op jit(solution)/shard_map/ppermute | solution.py:28
  107.8 26.0 %collective-permute-start.10 = (bf16[192,1024]{1,0:T(8,128)(2,1)S(1)}, bf16[192,1024]{1,0:T(8,128)(2,1)S(1)}, u32[]{:S(2)}, u32[]{:S(2)}) collective-permute-start(bf16[192,1024]{1,0:T(8,128)(2,1)S(1)} %get-tuple-element.22), channel_id=1, source_target_pairs={{0,16},{8,24},{16,0},{24,8},{1,17},{9,25},{17,1},{25,9},{2,18},{10... | collective-permute-start | bytes 1179656 | tf_op jit(solution)/shard_map/ppermute | solution.py:28
  117.7 0.8 copy-start.10
  118.5 15.5 %collective-permute-start.9 = (bf16[384,1024]{1,0:T(8,128)(2,1)S(1)}, bf16[384,1024]{1,0:T(8,128)(2,1)S(1)}, u32[]{:S(2)}, u32[]{:S(2)}) collective-permute-start(bf16[384,1024]{1,0:T(8,128)(2,1)S(1)} %pad_maximum_fusion.6), channel_id=1, source_target_pairs={{0,8},{8,0},{16,24},{24,16},{1,9},{9,1},{17,25},{25,17},{2,10},{10... | collective-permute-start | bytes 2359304 | tf_op jit(solution)/shard_map/ppermute | solution.py:28
  126.1 11.0 %copy-start.8 = (bf16[192,1024]{1,0:T(8,128)(2,1)}, bf16[192,1024]{1,0:T(8,128)(2,1)S(1)}, u32[]{:S(2)}) copy-start(bf16[192,1024]{1,0:T(8,128)(2,1)S(1)} %collective-permute-done.12) | copy-start | bytes 1179652
  126.2 8.8 %collective-permute-start.13 = (bf16[384,1024]{1,0:T(8,128)(2,1)S(1)}, bf16[384,1024]{1,0:T(8,128)(2,1)S(1)}, u32[]{:S(2)}, u32[]{:S(2)}) collective-permute-start(bf16[384,1024]{1,0:T(8,128)(2,1)S(1)} %pad_maximum_fusion.8), channel_id=1, source_target_pairs={{0,8},{8,0},{16,24},{24,16},{1,9},{9,1},{17,25},{25,17},{2,10},{10... | collective-permute-start | bytes 2359304 | tf_op jit(solution)/shard_map/ppermute | solution.py:28
  133.9 2.4 %collective-permute-start.11 = (bf16[384,1024]{1,0:T(8,128)(2,1)S(1)}, bf16[384,1024]{1,0:T(8,128)(2,1)S(1)}, u32[]{:S(2)}, u32[]{:S(2)}) collective-permute-start(bf16[384,1024]{1,0:T(8,128)(2,1)S(1)} %pad_maximum_fusion.7), channel_id=1, source_target_pairs={{0,8},{8,0},{16,24},{24,16},{1,9},{9,1},{17,25},{25,17},{2,10},{10... | collective-permute-start | bytes 2359304 | tf_op jit(solution)/shard_map/ppermute | solution.py:28
  135.0 5.7 %copy-start.14 = (bf16[192,1024]{1,0:T(8,128)(2,1)}, bf16[192,1024]{1,0:T(8,128)(2,1)S(1)}, u32[]{:S(2)}) copy-start(bf16[192,1024]{1,0:T(8,128)(2,1)S(1)} %get-tuple-element.33) | copy-start | bytes 1179652
  135.0 5.7 %copy-start.16 = (bf16[192,1024]{1,0:T(8,128)(2,1)}, bf16[192,1024]{1,0:T(8,128)(2,1)S(1)}, u32[]{:S(2)}) copy-start(bf16[192,1024]{1,0:T(8,128)(2,1)S(1)} %get-tuple-element.34) | copy-start | bytes 1179652
  153.9 1.5 copy-start.1
  155.4 1.5 copy-start.2
  156.9 44.7 %copy-start.20 = (s32[128,4]{0,1:T(4,128)S(1)}, s32[128,4]{0,1:T(4,128)}, u32[]{:S(2)}) copy-start(s32[128,4]{0,1:T(4,128)} %param.8) | copy-start | bytes 6148
  156.9 45.3 %copy-start.11 = (bf16[192,1024]{1,0:T(8,128)(2,1)S(1)}, bf16[192,1024]{1,0:T(8,128)(2,1)}, u32[]{:S(2)}) copy-start(bf16[192,1024]{1,0:T(8,128)(2,1)} %copy-done.10) | copy-start | bytes 1179652
  156.9 45.3 %copy-start.12 = (bf16[192,1024]{1,0:T(8,128)(2,1)S(1)}, bf16[192,1024]{1,0:T(8,128)(2,1)}, u32[]{:S(2)}) copy-start(bf16[192,1024]{1,0:T(8,128)(2,1)} %get-tuple-element.35) | copy-start | bytes 1179652
  156.9 45.3 %copy-start.13 = (bf16[192,1024]{1,0:T(8,128)(2,1)S(1)}, bf16[192,1024]{1,0:T(8,128)(2,1)}, u32[]{:S(2)}) copy-start(bf16[192,1024]{1,0:T(8,128)(2,1)} %get-tuple-element.36) | copy-start | bytes 1179652
  156.9 45.3 %copy-start.26 = (bf16[768,896]{1,0:T(8,128)(2,1)S(1)}, bf16[768,896]{1,0:T(8,128)(2,1)}, u32[]{:S(2)}) copy-start(bf16[768,896]{1,0:T(8,128)(2,1)} %copy-done.25) | copy-start | bytes 4128772
  202.2 3.3 %copy-start.9 = (bf16[192,1024]{1,0:T(8,128)(2,1)S(1)}, bf16[192,1024]{1,0:T(8,128)(2,1)}, u32[]{:S(2)}) copy-start(bf16[192,1024]{1,0:T(8,128)(2,1)} %copy-done.8) | copy-start | bytes 1179652
  202.2 3.2 %copy-start.15 = (bf16[192,1024]{1,0:T(8,128)(2,1)S(1)}, bf16[192,1024]{1,0:T(8,128)(2,1)}, u32[]{:S(2)}) copy-start(bf16[192,1024]{1,0:T(8,128)(2,1)} %copy-done.14) | copy-start | bytes 1179652
  202.2 3.2 %copy-start.17 = (bf16[192,1024]{1,0:T(8,128)(2,1)S(1)}, bf16[192,1024]{1,0:T(8,128)(2,1)}, u32[]{:S(2)}) copy-start(bf16[192,1024]{1,0:T(8,128)(2,1)} %copy-done.16) | copy-start | bytes 1179652
  202.2 3.2 %copy-start.24 = (bf16[768,896]{1,0:T(8,128)(2,1)S(1)}, bf16[768,896]{1,0:T(8,128)(2,1)}, u32[]{:S(2)}) copy-start(bf16[768,896]{1,0:T(8,128)(2,1)} %copy-done.23) | copy-start | bytes 4128772
  205.5 2.9 %copy-start.18 = (bf16[192,1024]{1,0:T(8,128)(2,1)S(1)}, bf16[192,1024]{1,0:T(8,128)(2,1)}, u32[]{:S(2)}) copy-start(bf16[192,1024]{1,0:T(8,128)(2,1)} %get-tuple-element.31) | copy-start | bytes 1179652
  205.5 2.9 %copy-start.19 = (bf16[192,1024]{1,0:T(8,128)(2,1)S(1)}, bf16[192,1024]{1,0:T(8,128)(2,1)}, u32[]{:S(2)}) copy-start(bf16[192,1024]{1,0:T(8,128)(2,1)} %get-tuple-element.32) | copy-start | bytes 1179652
where the time goes:
time: 213 us
  Pallas kernels  94 us (44%)
  waiting for transfers between devices  52.3 us (25%)
  matrix products  36.3 us (17%)
  local copies, waits for them, and re-layouts  14.5 us (7%)
  starting transfers between devices  9.27 us (4%)
  other arithmetic  5.14 us (2%)
    ppermute x14, waiting for transfers between devices, hop(): return lax.ppermute(v, 'dp', [(i, i ^ bit) for i in range(count)])  52.3 us
    pallas_call x1, Pallas kernels, all_rows(): pl.pallas_call(functools.partial(gather_kernel, experts // 2), out_shape=...  49.3 us
    pallas_call x1, Pallas kernels, sum_rows(): pl.pallas_call(functools.partial(scatter_kernel, lines), out_shape=[jax.S...  44.7 us
    dot_general x5, matrix products, dot_t(): lax.dot_general(a, b, (((0,), (0,)), ((), ())), preferred_element_type=F32)  22.1 us
    unnamed x56, local copies, waits for them, and re-layouts  12.1 us
    ppermute x14, starting transfers between devices, hop(): return lax.ppermute(v, 'dp', [(i, i ^ bit) for i in range(count)])  9.27 us
    dot_general x4, matrix products, dot(): return jnp.dot(a, b, preferred_element_type=F32)  8.87 us
    dot_general x2, matrix products, dot_nt(): lax.dot_general(a, b, (((1,), (1,)), ((), ())), preferred_element_type=F32)  5.36 us
  transfers between devices with their start and end apart: 14, of which 9 were waited for; matrix products, arithmetic and copies ran while one was open for 3% of the time, Pallas kernels for 0%

commit v1 on v0

--- a/solution.py
+++ b/solution.py
@@ -48,64 +48,212 @@
 VM = pl.BlockSpec(memory_space=pltpu.VMEM)
 
 
-def greet(z, y, lines):
+def greet(z, y, lines, dp_peers=()):
     barrier = pltpu.get_barrier_semaphore()
     me = z * 2 + y
 
-    def call(dev):
-        pl.semaphore_signal(barrier, inc=1, device_id={"expert": dev}, device_id_type=MESH)
-
-    call(me + 1 - 2 * y)
-    pl.when(z > 0)(lambda: call(me - 2))
-    pl.when(z < lines - 1)(lambda: call(me + 2))
-    peers = 1 + jnp.where(z > 0, 1, 0) + jnp.where(z < lines - 1, 1, 0)
+    def call(**dev):
+        pl.semaphore_signal(barrier, inc=1, device_id=dev, device_id_type=MESH)
+
+    call(expert=me + 1 - 2 * y)
+    for dev in dp_peers:
+        call(dp=dev)
+    pl.when(z > 0)(lambda: call(expert=me - 2))
+    pl.when(z < lines - 1)(lambda: call(expert=me + 2))
+    peers = 1 + len(dp_peers) + jnp.where(z > 0, 1, 0) + jnp.where(z < lines - 1, 1, 0)
     pl.semaphore_wait(barrier, peers)
 
 
-def gather_kernel(lines, *refs):
-    n = 3
-    own, full = refs[:n], refs[n:2 * n]
-    ssem, rsem, lsem = refs[2 * n:]
+def rows_dot(out, left, right, contract, rows):
+    @pl.loop(0, out.shape[0] // rows)
+    def _(i):
+        at = pl.ds(pl.multiple_of(i * rows, rows), rows)
+        out[at, :] = lax.dot_general(
+            left[at, :], right[...], (((1,), (contract,)), ((), ())), preferred_element_type=F32
+        ).astype(out.dtype)
+
+
+def front_kernel(lines, table, tok, cot, wg, wu, wd, hidden, gpg, upg, inner, xs, cs, pick, gate_out,
+                 tall, xall, call, part, cbuf, obuf, xbuf, fbuf, ssem, rsem, lsem, cs_sem, cr_sem,
+                 xs_sem, xr_sem, gxs, gxr, gcs, gcr):
+    own, full = (table, tok, cot), (tall, xall, call)
     me = lax.axis_index("expert")
+    d = lax.axis_index("dp")
     z, y = me // 2, me % 2
+    xc, cc = d // 2, d % 2
     partner = me + 1 - 2 * y
+    core, over = d + 1 - 2 * cc, d + 2 - 4 * xc
+    q = inner.shape[1]
+    tok_rows = tok.shape[0]
+    res = (hidden, gpg, upg)
+
+    def held(a, owner):
+        rows = own[a].shape[0]
+        return full[a].at[pl.ds(pl.multiple_of(owner * rows, rows), rows)]
 
     def move(a, way, owner, dev, src=None):
         return pltpu.make_async_remote_copy(
-            src_ref=full[a].at[owner] if src is None else src,
-            dst_ref=full[a].at[owner],
+            src_ref=held(a, owner) if src is None else src,
+            dst_ref=held(a, owner),
             send_sem=ssem.at[a, way, owner],
             recv_sem=rsem.at[a, owner],
             device_id={"expert": dev},
             device_id_type=MESH,
         )
 
-    greet(z, y, lines)
-    for a in range(n):
+    def begin(a):
         pl.when(z < lines - 1)(lambda: move(a, 0, me, me + 2, own[a]).start())
         pl.when(z > 0)(lambda: move(a, 1, me, me - 2, own[a]).start())
         move(a, 2, me, partner, own[a]).start()
-    local = [pltpu.make_async_copy(own[a], full[a].at[me], lsem.at[a]) for a in range(n)]
-    for copy in local:
-        copy.start()
-    for a in range(n):
-        for s in range(1, lines):
-            @pl.when(z >= s)
-            def _():
-                owner = me - 2 * s
-                move(a, 0, owner, partner).wait_recv()
-                pl.when(z < lines - 1)(lambda: move(a, 0, owner, me + 2).start())
-                move(a, 2, owner, partner).start()
-
-            @pl.when(z + s < lines)
-            def _():
-                owner = me + 2 * s
-                move(a, 1, owner, partner).wait_recv()
-                pl.when(z > 0)(lambda: move(a, 1, owner, me - 2).start())
-                move(a, 2, owner, partner).start()
-    for a in range(n):
+        pltpu.make_async_copy(own[a], held(a, me), lsem.at[a]).start()
+
+    def forward(a, s):
+        @pl.when(z >= s)
+        def _():
+            owner = me - 2 * s
+            move(a, 0, owner, partner).wait_recv()
+            pl.when(z < lines - 1)(lambda: move(a, 0, owner, me + 2).start())
+            move(a, 2, owner, partner).start()
+
+        @pl.when(z + s < lines)
+        def _():
+            owner = me + 2 * s
+            move(a, 1, owner, partner).wait_recv()
+            pl.when(z > 0)(lambda: move(a, 1, owner, me - 2).start())
+            move(a, 2, owner, partner).start()
+
+    def arrive(a):
         for line in range(lines):
             move(a, 2, line * 2 + 1 - y, partner).wait_recv()
+        pltpu.make_async_copy(own[a], held(a, me), lsem.at[a]).wait()
+
+    def dp_copy(src, dst, send, recv, dev):
+        return pltpu.make_async_remote_copy(
+            src_ref=src, dst_ref=dst, send_sem=send, recv_sem=recv,
+            device_id={"dp": dev}, device_id_type=MESH,
+        )
+
+    def to_core(m, i):
+        return dp_copy(part.at[m, pl.ds((2 * i + 1) * q, q)], cbuf.at[m, i], cs_sem.at[m, i], cr_sem.at[m, i], core)
+
+    def to_over(m):
+        return dp_copy(obuf.at[m], xbuf.at[m], xs_sem.at[m], xr_sem.at[m], over)
+
+    def block(m, i):
+        return inner.at[i] if m == 3 else res[m].at[pl.ds(i * q, q)]
+
+    def share_over(m):
+        return dp_copy(block(m, 0), block(m, 2), gxs.at[m], gxr.at[m], over)
+
+    def share_core(m, i):
+        return dp_copy(block(m, 2 * i), block(m, 2 * i + 1), gcs.at[m, i], gcr.at[m, i], core)
+
+    def send_sum(m):
+        for i in range(2):
+            to_core(m, i).wait_recv()
+        obuf[m] = (part[m, 2 * q:3 * q].astype(F32) + cbuf[m, 1].astype(F32)).astype(BF)
+        to_over(m).start()
+        fbuf[m] = part[m, :q].astype(F32) + cbuf[m, 0].astype(F32)
+
+    def take_sum(m):
+        to_over(m).wait_recv()
+        fbuf[m] = fbuf[m] + xbuf[m].astype(F32)
+
+    def share(m):
+        share_over(m).start()
+        share_core(m, 0).start()
+
+    greet(z, y, lines, (core, over))
+    begin(0)
+    begin(1)
+    for s in range(1, lines):
+        forward(0, s)
+    arrive(0)
+    tables = tall[...].reshape(2 * lines, 2 * lines, tok_rows)
+    chosen = lax.broadcasted_iota(jnp.int32, tables.shape, 1) == me
+    weight = jnp.sum(jnp.where(chosen, tables, 0.0), axis=1)
+    routed = weight > 0.0
+    upto = lax.broadcasted_iota(jnp.int32, (tok_rows, tok_rows), 0) <= lax.broadcasted_iota(
+        jnp.int32, (tok_rows, tok_rows), 1
+    )
+    count = jnp.dot(
+        jnp.where(routed, 1.0, 0.0), jnp.where(upto, 1.0, 0.0), preferred_element_type=F32
+    )
+    forward(1, 1)
+    begin(2)
+    gates = [jnp.zeros((q, 1), F32) for _ in range(4)]
+    before = jnp.zeros((1, 1), F32)
+    for src in range(2 * lines):
+        row = slice(src, src + 1)
+        rank = jnp.where(routed[row], count[row] - 1.0 + before, -1.0)
+        before = before + count[row, tok_rows - 1:]
+        for b in range(4):
+            owner = (xc + b // 2) % 2 * 2 + (cc + b % 2) % 2
+            ids = (lax.broadcasted_iota(jnp.int32, (q, tok_rows), 0) + owner * q).astype(F32)
+            hit = ids == rank
+            pick[b * q:(b + 1) * q, src * tok_rows:(src + 1) * tok_rows] = jnp.where(hit, 1.0, 0.0).astype(BF)
+            gates[b] = gates[b] + jnp.sum(jnp.where(hit, weight[row], 0.0), axis=1, keepdims=True)
+        if src == 3:
+            forward(1, 2)
+    for b in range(4):
+        gate_out[b * q:(b + 1) * q, :] = jnp.broadcast_to(gates[b], (q, 128))
+    for s in range(3, lines):
+        forward(1, s)
+    arrive(1)
+    rows_dot(xs, pick, xall, 0, 2 * q)
+    forward(2, 1)
+    rows_dot(part.at[0], xs, wg, 0, 2 * q)
+    for i in range(2):
+        to_core(0, i).start()
+    forward(2, 2)
+    rows_dot(part.at[1], xs, wu, 0, 2 * q)
+    for i in range(2):
+        to_core(1, i).start()
+    send_sum(0)
+    send_sum(1)
+    for s in range(3, lines):
+        forward(2, s)
+    take_sum(0)
+    take_sum(1)
+    gate_pre, up_pre = fbuf[0], fbuf[1]
+    hidden[:q, :] = (gate_pre * jax.nn.sigmoid(gate_pre) * up_pre).astype(BF)
+    share(0)
+    arrive(2)
+    rows_dot(cs, pick, call, 0, 2 * q)
+    rows_dot(part.at[2], cs, wd, 1, 2 * q)
+    for i in range(2):
+        to_core(2, i).start()
+    send_sum(2)
+    share_over(0).wait_recv()
+    share_core(0, 1).start()
+    take_sum(2)
+
+    gate_pre, up_pre, raw = fbuf[0], fbuf[1], fbuf[2]
+    sig = jax.nn.sigmoid(gate_pre)
+    active = gate_pre * sig
+    grad = raw * gate_out[:q, :1]
+    gpg[:q, :] = (grad * up_pre * sig * (1.0 + gate_pre * (1.0 - sig))).astype(BF)
+    share(1)
+    upg[:q, :] = (grad * active).astype(BF)
+    share(2)
+    inner[0] = jnp.broadcast_to(jnp.sum(active * up_pre * raw, axis=1, keepdims=True), (q, 128))
+    share(3)
+    for m in (1, 2, 3):
+        share_over(m).wait_recv()
+        share_core(m, 1).start()
+    for m in range(4):
+        for i in range(2):
+            share_core(m, i).wait_recv()
+    for m in range(4):
+        share_over(m).wait_send()
+        for i in range(2):
+            share_core(m, i).wait_send()
+    for m in range(3):
+        to_over(m).wait_send()
+        for i in range(2):
+            to_core(m, i).wait_send()
+    for a in range(3):
+        for line in range(lines):
             move(a, 2, line * 2 + y, partner).wait_send()
 
             @pl.when((line <= z) & (z < lines - 1))
@@ -115,26 +263,47 @@
             @pl.when((line >= z) & (z > 0))
             def _():
                 move(a, 1, line * 2 + y, partner).wait_send()
-    for copy in local:
-        copy.wait()
-
-
-def all_rows(experts, *blocks):
-    n = len(blocks)
+
+
+def front(experts, slots, table, tok, cot, wg, wu, wd):
+    tok_rows, quarter = tok.shape
+    width, q = wd.shape[0], slots // 4
+    sds = jax.ShapeDtypeStruct
+    dma = pltpu.SemaphoreType.DMA
+    blocks = pltpu.VMEM((3, q, width), BF)
     return pl.pallas_call(
-        functools.partial(gather_kernel, experts // 2),
-        out_shape=[jax.ShapeDtypeStruct((experts,) + b.shape, b.dtype) for b in blocks],
-        in_specs=[VM] * n,
-        out_specs=[VM] * n,
+        functools.partial(front_kernel, experts // 2),
+        out_shape=[sds((slots, width), BF)] * 3
+        + [sds((4, q, 128), F32)]
+        + [sds((slots, quarter), BF)] * 2
+        + [sds((slots, experts * tok_rows), BF), sds((slots, 128), F32)],
+        in_specs=[VM] * 6,
+        out_specs=[VM] * 8,
         scratch_shapes=[
-            pltpu.SemaphoreType.DMA((n, 3, experts)),
-            pltpu.SemaphoreType.DMA((n, experts)),
-            pltpu.SemaphoreType.DMA((n,)),
+            pltpu.VMEM((experts * experts, tok_rows), F32),
+            pltpu.VMEM((experts * tok_rows, quarter), BF),
+            pltpu.VMEM((experts * tok_rows, quarter), BF),
+            pltpu.VMEM((3, slots, width), BF),
+            pltpu.VMEM((3, 2, q, width), BF),
+            blocks,
+            blocks,
+            pltpu.VMEM((3, q, width), F32),
+            dma((3, 3, experts)),
+            dma((3, experts)),
+            dma((3,)),
+            dma((3, 2)),
+            dma((3, 2)),
+            dma((3,)),
+            dma((3,)),
+            dma((4,)),
+            dma((4,)),
+            dma((4, 2)),
+            dma((4, 2)),
         ],
         compiler_params=pltpu.CompilerParams(
-            collective_id=0, has_side_effects=True, vmem_limit_bytes=40 << 20
+            collective_id=0, has_side_effects=True, vmem_limit_bytes=56 << 20
         ),
-    )(*blocks)
+    )(table, tok, cot, wg, wu, wd)
 
 
 def scatter_kernel(lines, *refs):
@@ -248,48 +417,50 @@
     table = jnp.sum(jnp.where(chosen, gates[:, :, None], 0.0), axis=1)
     near = experts == 8
     if near:
-        tables, x, c = all_rows(experts, table.T, tokens, cotangent)
-        weight = lax.dynamic_index_in_dim(tables, me, axis=1, keepdims=False)
-        x = x.reshape(experts * tok_rows, quarter)
-        c = c.reshape(experts * tok_rows, quarter)
+        hidden, gpg, upg, inner, xs, cs, pick, slot_gate = front(
+            experts, slots, table.T, tokens, cotangent, wg, wu, wd
+        )
+        slot_gate = slot_gate[:, 0]
+        inner = inner[:, :, :1].reshape(slots, 1)
     else:
         weight = lax.all_to_all(table.T, "expert", split_axis=0, concat_axis=0, tiled=True)
         x = lax.all_gather(tokens, "expert", axis=0, tiled=True)
         c = lax.all_gather(cotangent, "expert", axis=0, tiled=True)
-    weight = weight.reshape(experts * tok_rows)
-
-    routed = weight > 0.0
-    rank = jnp.cumsum(routed.astype(jnp.int32)) - 1
-    rank = jnp.where(routed, rank, -1)
-    place = jnp.arange(slots, dtype=jnp.int32)
-    place = (place // q ^ d) * q + place % q
-    hit = place[:, None] == rank[None, :]
-    pick = hit.astype(BF)
-    slot_gate = jnp.sum(jnp.where(hit, weight[None, :], 0.0), axis=1)
-
-    xs = dot(pick, x).astype(BF)
-    gate_pre = reduce_rows(dot(xs, wg).astype(BF))
-    up_pre = reduce_rows(dot(xs, wu).astype(BF))
-    cs = dot(pick, c).astype(BF)
-    raw_grad = reduce_rows(dot_nt(cs, wd).astype(BF))
-
-    own_gate = slot_gate[:q, None]
-    sig = jax.nn.sigmoid(gate_pre)
-    active = gate_pre * sig
-    hidden32 = active * up_pre
-    hidden = gather_rows(hidden32.astype(BF))
-    gate_inner = jnp.sum(hidden32 * raw_grad, axis=1)
-    hidden_grad = raw_grad * own_gate
-    gpg = gather_rows((hidden_grad * up_pre * sig * (1.0 + gate_pre * (1.0 - sig))).astype(BF))
-    upg = gather_rows((hidden_grad * active).astype(BF))
+        weight = weight.reshape(experts * tok_rows)
+
+        routed = weight > 0.0
+        rank = jnp.cumsum(routed.astype(jnp.int32)) - 1
+        rank = jnp.where(routed, rank, -1)
+        place = jnp.arange(slots, dtype=jnp.int32)
+        place = (place // q ^ d) * q + place % q
+        hit = place[:, None] == rank[None, :]
+        pick = hit.astype(BF)
+        slot_gate = jnp.sum(jnp.where(hit, weight[None, :], 0.0), axis=1)
+
+        xs = dot(pick, x).astype(BF)
+        gate_pre = reduce_rows(dot(xs, wg).astype(BF))
+        up_pre = reduce_rows(dot(xs, wu).astype(BF))
+        cs = dot(pick, c).astype(BF)
+        raw_grad = reduce_rows(dot_nt(cs, wd).astype(BF))
+
+        own_gate = slot_gate[:q, None]
+        sig = jax.nn.sigmoid(gate_pre)
+        active = gate_pre * sig
+        hidden32 = active * up_pre
+        hidden = gather_rows(hidden32.astype(BF))
+        gate_inner = jnp.sum(hidden32 * raw_grad, axis=1)
+        hidden_grad = raw_grad * own_gate
+        gpg = gather_rows((hidden_grad * up_pre * sig * (1.0 + gate_pre * (1.0 - sig))).astype(BF))
+        upg = gather_rows((hidden_grad * active).astype(BF))
+
+        inner = gather_rows(gate_inner[:, None])
 
     out = (dot(hidden, wd) * slot_gate[:, None]).astype(BF)
     out = dot_t(pick, out).astype(BF)
     pair = (dot_nt(gpg, wg) + dot_nt(upg, wu)).astype(BF)
     pair = dot_t(pick, pair).astype(BF)
 
-    inner = gather_rows(gate_inner[:, None])
-    inner = jnp.sum(jnp.where(hit, inner, 0.0), axis=0).reshape(experts, tok_rows)
+    inner = jnp.sum(jnp.where(pick > 0, inner, 0.0), axis=0).reshape(experts, tok_rows)
     if near:
         mine = (labels == me)[None, :, None]
         inner, mixed, token_grad = sum_rows(

time: 213 us -> 187 us (0.88)
  Pallas kernels: 94 us -> 151 us
  waiting for transfers between devices: 52.3 us -> 0 us
  matrix products: 36.3 us -> 26.8 us
  starting transfers between devices: 9.27 us -> 0 us
  local copies, waits for them, and re-layouts: 14.5 us -> 5.35 us
  other arithmetic: 5.14 us -> 2.49 us
    pallas_call x1, Pallas kernels: 49.3 us -> 106 us  [front(): pl.pallas_call(functools.partial(front_kernel, experts // 2), out_shape=[...]
    ppermute x14 -> x0, waiting for transfers between devices: 52.3 us -> none  [hop(): return lax.ppermute(v, 'dp', [(i, i ^ bit) for i in range(count)])]
    ppermute x14 -> x0, starting transfers between devices: 9.27 us -> none  [hop(): return lax.ppermute(v, 'dp', [(i, i ^ bit) for i in range(count)])]
    unnamed x56 -> x20, local copies, waits for them, and re-layouts: 12.1 us -> 2.9 us
    dot_general x4 -> x0, matrix products: 8.87 us -> none  [dot(): return jnp.dot(a, b, preferred_element_type=F32)]
    dot_general x2 -> x1, matrix products: 5.36 us -> 4.91 us  [dot_nt(): lax.dot_general(a, b, (((1,), (1,)), ((), ())), preferred_element_type=F32)]
  transfers between devices with their start and end apart: 14 -> 0, of which waited for: 9 -> 0; matrix products, arithmetic and copies ran while one was open for 3% -> 0% of each run, Pallas kernels for 0% -> 0%
where the time goes in v1:
time: 187 us; the launch traced here: 186 us
  Pallas kernels  151 us (81%)
  matrix products  26.8 us (14%)
  local copies, waits for them, and re-layouts  5.35 us (3%)
  other arithmetic  2.49 us (1%)
    pallas_call x1, Pallas kernels, front(): pl.pallas_call(functools.partial(front_kernel, experts // 2), out_shape=[...  106 us
    pallas_call x1, Pallas kernels, sum_rows(): pl.pallas_call(functools.partial(scatter_kernel, lines), out_shape=[jax.S...  44.7 us
    dot_general x5, matrix products, dot_t(): lax.dot_general(a, b, (((0,), (0,)), ((), ())), preferred_element_type=F32)  21.9 us
    dot_general x1, matrix products, dot_nt(): lax.dot_general(a, b, (((1,), (1,)), ((), ())), preferred_element_type=F32)  4.91 us

profile of v1, /device:TPU:0, one launch (start us, length us, event | category | flops | bytes accessed | tf_op | source)
XLA Modules:
  0.0 186.3 jit_solution(10444808837004375599)
XLA Ops:
  0.6 1.3 select_reduce_fusion.2
  1.9 0.0 copy-start.1
  1.9 106.3 %shard_map.118 = (bf16[768,1024]{1,0:T(8,128)(2,1)}, bf16[768,1024]{1,0:T(8,128)(2,1)}, bf16[768,1024]{1,0:T(8,128)(2,1)}, f32[4,192,128]{2,1,0:T(8,128)}, bf16[...) custom-call(f32[8,128]{1,0:T(8,128)} %bitcast.39, ...), custom_call_target="tpu_custom_call" | custom-call | tf_op jit(solution)/shard_map/pallas_call | solution.py:274
  108.2 0.0 copy-done.1
  108.3 0.0 copy-start.2
  108.3 4.9 %fusion.5 = f32[768,896]{1,0:T(8,128)} fusion(bf16[768,1024]{1,0:T(8,128)(2,1)} %get-tuple-element.21, bf16[1,896,1024]{2,1,0:T(8,128)(2,1)S(1)} %copy-done.1), kind=kOutput, calls=%fused_computation.19 | convolution fusion | flops 1409286144 | bytes 6160384 | tf_op jit(solution)/shard_map/dot_general | solution.py:23
  113.2 0.0 copy-done.2
  113.2 6.3 %convolution_convert_fusion = bf16[1024,896]{1,0:T(8,128)(2,1)S(1)} fusion(bf16[768,1024]{1,0:T(8,128)(2,1)S(1)} %copy-done.2, f32[768,896]{1,0:T(8,128)} %fusion.5, bf16[768,1024]{1,0:T(8,128)(2,1)} %get-tuple-element.22, bf16[1,896,1024]{2,1,0:T(8,128)(2,1)} %param.11), kind=kOutput, calls=%fused_computation.7 | convolution fusion | flops 2820866048 | bytes 9568256 | tf_op jit(solution)/shard_map/dot_general | solution.py:19
  119.5 1.2 slice_reduce_fusion
  120.6 6.6 %convolution_convert_fusion.1 = bf16[1024,896]{1,0:T(8,128)(2,1)} fusion(bf16[768,1024]{1,0:T(8,128)(2,1)S(1)} %copy-done.2, bf16[768,1024]{1,0:T(8,128)(2,1)} %get-tuple-element.19, f32[768]{0:T(1024)S(1)} %slice_reduce_fusion, bf16[1,1024,896]{2,1,0:T(8,128)(2,1)} %param.12), kind=kOutput, calls=%fused_computation.8 | convolution fusion | flops 2820866048 | bytes 6818816 | tf_op jit(solution)/shard_map/dot_general | solution.py:19
  127.3 1.2 slice_reduce_fusion.1
  128.5 0.1 broadcast_in_dim.75
  128.6 0.5 select_reduce_fusion
  129.1 0.1 broadcast_select_fusion.refs_0_
  129.2 0.0 copy-start
  129.2 1.5 copy-done
  130.7 0.0 copy-start.3
  130.7 0.0 copy-start.6
  130.7 0.0 copy-start.8
  130.7 44.7 %shard_map.119 = (f32[8,128]{1,0:T(8,128)S(1)}, bf16[128,896]{1,0:T(8,128)(2,1)S(1)}, bf16[128,896]{1,0:T(8,128)(2,1)S(1)}) custom-call(f32[8,8,128]{2,1,0:T(8,128)S(1)} %broadcast_select_fusion.refs_0_, bf16[8,128,896]{2,1,0:T(8,128)(2,1)S(1)} %bitcast.33, bf16[8,128,896]{2,1,0:T(8,128)(2,1)S(1)} %bitcast.32), custom_call_target="tpu_custom_call" | custom-call | tf_op jit(solution)/shard_map/pallas_call | solution.py:392
  175.4 0.0 copy-done.3
  175.4 0.6 select_reduce_fusion.1
  176.0 0.0 copy-done.6
  176.0 0.0 copy-done.8
  176.0 0.0 copy-start.5
  176.0 0.0 copy-start.7
  176.0 3.2 %convert_bitcast_fusion = bf16[1,1024,896]{2,1,0:T(8,128)(2,1)} fusion(bf16[768,896]{1,0:T(8,128)(2,1)S(1)} %copy-done.8, bf16[768,1024]{1,0:T(8,128)(2,1)S(1)} %copy-done.6, f32[768]{0:T(1024)S(1)} %slice_reduce_fusion), kind=kOutput, calls=%fused_computation.4 | convolution fusion | flops 1412562944 | bytes 4787200 | tf_op jit(solution)/shard_map/dot_general | solution.py:19
  179.2 0.0 copy-done.5
  179.2 0.0 copy-done.7
  179.2 0.0 copy-start.4
  179.2 2.9 %convert_bitcast_fusion.1 = bf16[1,896,1024]{2,1,0:T(8,128)(2,1)} fusion(bf16[768,896]{1,0:T(8,128)(2,1)S(1)} %copy-done.7, bf16[768,1024]{1,0:T(8,128)(2,1)S(1)} %copy-done.5), kind=kOutput, calls=%fused_computation.5 | convolution fusion | flops 1410203648 | bytes 4784128 | tf_op jit(solution)/shard_map/dot_general | solution.py:19
  182.1 0.0 copy-done.4
  182.1 2.9 %convert_bitcast_fusion.2 = bf16[1,896,1024]{2,1,0:T(8,128)(2,1)} fusion(bf16[768,896]{1,0:T(8,128)(2,1)S(1)} %copy-done.7, bf16[768,1024]{1,0:T(8,128)(2,1)S(1)} %copy-done.4), kind=kOutput, calls=%fused_computation.6 | convolution fusion | flops 1410203648 | bytes 4784128 | tf_op jit(solution)/shard_map/dot_general | solution.py:19
  185.0 0.7 copy.21
  185.6 0.7 copy.22
  (1 shorter events, 0.0 us)
Async XLA Ops:
  1.9 106.3 %copy-start.1 = (bf16[1,896,1024]{2,1,0:T(8,128)(2,1)S(1)}, bf16[1,896,1024]{2,1,0:T(8,128)(2,1)}, u32[]{:S(2)}) copy-start(bf16[1,896,1024]{2,1,0:T(8,128)(2,1)} %param.10) | copy-start | bytes 5505028
  108.3 4.9 %copy-start.2 = (bf16[768,1024]{1,0:T(8,128)(2,1)S(1)}, bf16[768,1024]{1,0:T(8,128)(2,1)}, u32[]{:S(2)}) copy-start(bf16[768,1024]{1,0:T(8,128)(2,1)} %get-tuple-element.17) | copy-start | bytes 4718596
  129.2 1.5 copy-start
  130.7 44.7 %copy-start.3 = (s32[128,4]{0,1:T(4,128)S(1)}, s32[128,4]{0,1:T(4,128)}, u32[]{:S(2)}) copy-start(s32[128,4]{0,1:T(4,128)} %param.8) | copy-start | bytes 6148
  130.7 45.3 %copy-start.6 = (bf16[768,1024]{1,0:T(8,128)(2,1)S(1)}, bf16[768,1024]{1,0:T(8,128)(2,1)}, u32[]{:S(2)}) copy-start(bf16[768,1024]{1,0:T(8,128)(2,1)} %get-tuple-element.19) | copy-start | bytes 4718596
  130.7 45.3 %copy-start.8 = (bf16[768,896]{1,0:T(8,128)(2,1)S(1)}, bf16[768,896]{1,0:T(8,128)(2,1)}, u32[]{:S(2)}) copy-start(bf16[768,896]{1,0:T(8,128)(2,1)} %get-tuple-element.27) | copy-start | bytes 4128772
  176.0 3.2 %copy-start.5 = (bf16[768,1024]{1,0:T(8,128)(2,1)S(1)}, bf16[768,1024]{1,0:T(8,128)(2,1)}, u32[]{:S(2)}) copy-start(bf16[768,1024]{1,0:T(8,128)(2,1)} %get-tuple-element.22) | copy-start | bytes 4718596
  176.0 3.2 %copy-start.7 = (bf16[768,896]{1,0:T(8,128)(2,1)S(1)}, bf16[768,896]{1,0:T(8,128)(2,1)}, u32[]{:S(2)}) copy-start(bf16[768,896]{1,0:T(8,128)(2,1)} %get-tuple-element.26) | copy-start | bytes 4128772
  179.2 2.9 %copy-start.4 = (bf16[768,1024]{1,0:T(8,128)(2,1)S(1)}, bf16[768,1024]{1,0:T(8,128)(2,1)}, u32[]{:S(2)}) copy-start(bf16[768,1024]{1,0:T(8,128)(2,1)} %get-tuple-element.21) | copy-start | bytes 4718596

commit v2 on v1

--- a/solution.py
+++ b/solution.py
@@ -73,9 +73,26 @@
         ).astype(out.dtype)
 
 
-def front_kernel(lines, table, tok, cot, wg, wu, wd, hidden, gpg, upg, inner, xs, cs, pick, gate_out,
-                 tall, xall, call, part, cbuf, obuf, xbuf, fbuf, ssem, rsem, lsem, cs_sem, cr_sem,
-                 xs_sem, xr_sem, gxs, gxr, gcs, gcr):
+def cols_dot(out, left, right, cuts):
+    for lo, hi in cuts:
+        out[lo:hi, :] = lax.dot_general(
+            left[:, lo:hi], right[...], (((0,), (0,)), ((), ())), preferred_element_type=F32
+        ).astype(out.dtype)
+
+
+def halves(width):
+    cut = (width // 2 + 127) // 128 * 128
+    return ((0, cut), (cut, width))
+
+
+def layer_kernel(lines, table, tok, cot, wg, wu, wd, inner_out, mixed, token_grad, wg_grad, wu_grad, wd_grad,
+                 hidden, gpg, upg, inner, xs, cs, pick, gate_out,
+                 tall, xall, call, part, cbuf, obuf, xbuf, fbuf, mid, scaled, inner_all, out_all, pair_all,
+                 yb0, yb1, yb2, ub0, ub1, ub2, db0, db1, db2, sb0, sb1, sb2,
+                 ssem, rsem, lsem, cs_sem, cr_sem,
+                 xs_sem, xr_sem, gxs, gxr, gcs, gcr, ysend, yrecv, zsend, urecv, drecv):
+    dense, out = (inner_all, out_all, pair_all), (inner_out, mixed, token_grad)
+    ybuf, ubuf, dbuf, sbuf = (yb0, yb1, yb2), (ub0, ub1, ub2), (db0, db1, db2), (sb0, sb1, sb2)
     own, full = (table, tok, cot), (tall, xall, call)
     me = lax.axis_index("expert")
     d = lax.axis_index("dp")
@@ -162,6 +179,83 @@
     def share(m):
         share_over(m).start()
         share_core(m, 0).start()
+
+    def chunk(a, owner):
+        rows = out[a].shape[0]
+        return pl.ds(pl.multiple_of(owner * rows, rows), rows)
+
+    def across(a, line):
+        return pltpu.make_async_remote_copy(
+            src_ref=dense[a].at[chunk(a, line * 2 + 1 - y)],
+            dst_ref=ybuf[a].at[line],
+            send_sem=ysend.at[a, line],
+            recv_sem=yrecv.at[a, line],
+            device_id={"expert": partner},
+            device_id_type=MESH,
+        )
+
+    def along(a, line, up):
+        return pltpu.make_async_remote_copy(
+            src_ref=sbuf[a].at[line],
+            dst_ref=(ubuf if up else dbuf)[a].at[line],
+            send_sem=zsend.at[a, line],
+            recv_sem=(urecv if up else drecv).at[a, line],
+            device_id={"expert": me + 2 if up else me - 2},
+            device_id_type=MESH,
+        )
+
+    def base(a, line):
+        across(a, line).wait_recv()
+        return dense[a][chunk(a, line * 2 + y), :].astype(F32) + ybuf[a][line].astype(F32)
+
+    def return_begin(a):
+        for s in range(lines - 1, 0, -1):
+            pl.when(z + s < lines)(lambda: across(a, z + s).start())
+            pl.when(z >= s)(lambda: across(a, z - s).start())
+        across(a, z).start()
+
+    def return_step(a, s):
+        @pl.when(z + s < lines)
+        def _():
+            line = z + s
+            sbuf[a][line] = base(a, line).astype(sbuf[a].dtype)
+
+            @pl.when(z > 0)
+            def _():
+                along(a, line, True).wait_recv()
+                sbuf[a][line] = (
+                    sbuf[a][line].astype(F32) + ubuf[a][line].astype(F32)
+                ).astype(sbuf[a].dtype)
+
+            along(a, line, True).start()
+
+        @pl.when(z >= s)
+        def _():
+            line = z - s
+            sbuf[a][line] = base(a, line).astype(sbuf[a].dtype)
+
+            @pl.when(z < lines - 1)
+            def _():
+                along(a, line, False).wait_recv()
+                sbuf[a][line] = (
+                    sbuf[a][line].astype(F32) + dbuf[a][line].astype(F32)
+                ).astype(sbuf[a].dtype)
+
+            along(a, line, False).start()
+
+    def return_end(a):
+        pl.when(z > 0)(lambda: along(a, z, True).wait_recv())
+        pl.when(z < lines - 1)(lambda: along(a, z, False).wait_recv())
+        total = base(a, z)
+        total = total + jnp.where(z > 0, ubuf[a][z].astype(F32), 0.0)
+        total = total + jnp.where(z < lines - 1, dbuf[a][z].astype(F32), 0.0)
+        out[a][...] = total.astype(out[a].dtype)
+        for line in range(lines):
+            across(a, line).wait_send()
+            pl.when(z != line)(lambda: along(a, line, True).wait_send())
+
+    def nt(left, right):
+        return lax.dot_general(left, right, (((1,), (1,)), ((), ())), preferred_element_type=F32)
 
     greet(z, y, lines, (core, over))
     begin(0)
@@ -224,8 +318,28 @@
     for i in range(2):
         to_core(2, i).start()
     send_sum(2)
-    share_over(0).wait_recv()
-    share_core(0, 1).start()
+
+    def finish(m):
+        share_over(m).wait_recv()
+        share_core(m, 1).start()
+
+    def whole(m):
+        for i in range(2):
+            share_core(m, i).wait_recv()
+
+    finish(0)
+    whole(0)
+
+    @pl.loop(0, 2)
+    def _(i):
+        at = pl.ds(pl.multiple_of(i * 2 * q, 2 * q), 2 * q)
+        mid[at, :] = (
+            jnp.dot(hidden[at, :], wd[...], preferred_element_type=F32) * gate_out[at, :1]
+        ).astype(BF)
+        scaled[at, :] = (hidden[at, :].astype(F32) * gate_out[at, :1]).astype(BF)
+
+    cols_dot(out_all, pick, mid, halves(pick.shape[1]))
+    return_begin(1)
     take_sum(2)
 
     gate_pre, up_pre, raw = fbuf[0], fbuf[1], fbuf[2]
@@ -238,12 +352,43 @@
     share(2)
     inner[0] = jnp.broadcast_to(jnp.sum(active * up_pre * raw, axis=1, keepdims=True), (q, 128))
     share(3)
-    for m in (1, 2, 3):
-        share_over(m).wait_recv()
-        share_core(m, 1).start()
-    for m in range(4):
-        for i in range(2):
-            share_core(m, i).wait_recv()
+    cols_dot(wd_grad, scaled, cs, halves(scaled.shape[1]))
+    return_step(1, lines - 1)
+    finish(1)
+    for s in range(lines - 2, 0, -1):
+        return_step(1, s)
+    finish(2)
+    finish(3)
+    whole(1)
+    whole(2)
+
+    @pl.loop(0, 2)
+    def _(i):
+        at = pl.ds(pl.multiple_of(i * 2 * q, 2 * q), 2 * q)
+        mid[at, :] = (nt(gpg[at, :], wg[...]) + nt(upg[at, :], wu[...])).astype(BF)
+
+    cols_dot(pair_all, pick, mid, halves(pick.shape[1]))
+    return_begin(2)
+    whole(3)
+    sums = jnp.zeros((1, pick.shape[1]), F32)
+    for b in range(4):
+        sums = sums + jnp.sum(
+            pick[b * q:(b + 1) * q, :].astype(F32) * inner[b][:, :1], axis=0, keepdims=True
+        )
+    for dst in range(2 * lines):
+        row = sums[:, dst * tok_rows:(dst + 1) * tok_rows]
+        mine = lax.broadcasted_iota(jnp.int32, (2 * lines, tok_rows), 0) == me
+        inner_all[dst * 2 * lines:(dst + 1) * 2 * lines, :] = jnp.where(mine, row, 0.0)
+    return_begin(0)
+    cols_dot(wg_grad, xs, gpg, halves(xs.shape[1]))
+    for s in range(lines - 1, 0, -1):
+        return_step(2, s)
+        return_step(0, s)
+        if s == lines - 1:
+            cols_dot(wu_grad, xs, upg, halves(xs.shape[1]))
+    return_end(1)
+    return_end(0)
+    return_end(2)
     for m in range(4):
         share_over(m).wait_send()
         for i in range(2):
@@ -265,21 +410,28 @@
                 move(a, 1, line * 2 + y, partner).wait_send()
 
 
-def front(experts, slots, table, tok, cot, wg, wu, wd):
+def layer(experts, slots, table, tok, cot, wg, wu, wd):
     tok_rows, quarter = tok.shape
     width, q = wd.shape[0], slots // 4
+    half = [pltpu.VMEM((experts // 2,) + b.shape, b.dtype) for b in (table, tok, tok)]
     sds = jax.ShapeDtypeStruct
     dma = pltpu.SemaphoreType.DMA
     blocks = pltpu.VMEM((3, q, width), BF)
     return pl.pallas_call(
-        functools.partial(front_kernel, experts // 2),
-        out_shape=[sds((slots, width), BF)] * 3
-        + [sds((4, q, 128), F32)]
-        + [sds((slots, quarter), BF)] * 2
-        + [sds((slots, experts * tok_rows), BF), sds((slots, 128), F32)],
+        functools.partial(layer_kernel, experts // 2),
+        out_shape=[sds(table.shape, F32), sds(tok.shape, BF), sds(tok.shape, BF)]
+        + [sds(w.shape, BF) for w in (wg, wu, wd)],
         in_specs=[VM] * 6,
-        out_specs=[VM] * 8,
+        out_specs=[VM] * 6,
         scratch_shapes=[
+            pltpu.VMEM((slots, width), BF),
+            pltpu.VMEM((slots, width), BF),
+            pltpu.VMEM((slots, width), BF),
+            pltpu.VMEM((4, q, 128), F32),
+            pltpu.VMEM((slots, quarter), BF),
+            pltpu.VMEM((slots, quarter), BF),
+            pltpu.VMEM((slots, experts * tok_rows), BF),
+            pltpu.VMEM((slots, 128), F32),
             pltpu.VMEM((experts * experts, tok_rows), F32),
             pltpu.VMEM((experts * tok_rows, quarter), BF),
             pltpu.VMEM((experts * tok_rows, quarter), BF),
@@ -288,6 +440,14 @@
             blocks,
             blocks,
             pltpu.VMEM((3, q, width), F32),
+            pltpu.VMEM((slots, quarter), BF),
+            pltpu.VMEM((slots, width), BF),
+            pltpu.VMEM((experts * experts, tok_rows), F32),
+            pltpu.VMEM((experts * tok_rows, quarter), BF),
+            pltpu.VMEM((experts * tok_rows, quarter), BF),
+        ]
+        + half * 4
+        + [
             dma((3, 3, experts)),
             dma((3, experts)),
             dma((3,)),
@@ -299,106 +459,12 @@
             dma((4,)),
             dma((4, 2)),
             dma((4, 2)),
-        ],
+        ]
+        + [dma((3, experts // 2))] * 5,
         compiler_params=pltpu.CompilerParams(
-            collective_id=0, has_side_effects=True, vmem_limit_bytes=56 << 20
+            collective_id=0, has_side_effects=True, vmem_limit_bytes=60 << 20
         ),
     )(table, tok, cot, wg, wu, wd)
-
-
-def scatter_kernel(lines, *refs):
-    n = 3
-    full, out = refs[:n], refs[n:2 * n]
-    ybuf, ubuf, dbuf, sbuf = (refs[(2 + i) * n:(3 + i) * n] for i in range(4))
-    ysend, yrecv, zsend, urecv, drecv = refs[6 * n:]
-    me = lax.axis_index("expert")
-    z, y = me // 2, me % 2
-    partner = me + 1 - 2 * y
-
-    def across(a, line):
-        return pltpu.make_async_remote_copy(
-            src_ref=full[a].at[line * 2 + 1 - y],
-            dst_ref=ybuf[a].at[line],
-            send_sem=ysend.at[a, line],
-            recv_sem=yrecv.at[a, line],
-            device_id={"expert": partner},
-            device_id_type=MESH,
-        )
-
-    def along(a, line, up):
-        return pltpu.make_async_remote_copy(
-            src_ref=sbuf[a].at[line],
-            dst_ref=(ubuf if up else dbuf)[a].at[line],
-            send_sem=zsend.at[a, line],
-            recv_sem=(urecv if up else drecv).at[a, line],
-            device_id={"expert": me + 2 if up else me - 2},
-            device_id_type=MESH,
-        )
-
-    def base(a, line):
-        across(a, line).wait_recv()
-        return full[a][line * 2 + y].astype(F32) + ybuf[a][line].astype(F32)
-
-    greet(z, y, lines)
-    for a in range(n):
-        for s in range(lines - 1, 0, -1):
-            pl.when(z + s < lines)(lambda: across(a, z + s).start())
-            pl.when(z >= s)(lambda: across(a, z - s).start())
-        across(a, z).start()
-    for a in range(n):
-        for s in range(lines - 1, 0, -1):
-            @pl.when(z + s < lines)
-            def _():
-                line = z + s
-                sbuf[a][line] = base(a, line).astype(sbuf[a].dtype)
-
-                @pl.when(z > 0)
-                def _():
-                    along(a, line, True).wait_recv()
-                    sbuf[a][line] = (
-                        sbuf[a][line].astype(F32) + ubuf[a][line].astype(F32)
-                    ).astype(sbuf[a].dtype)
-
-                along(a, line, True).start()
-
-            @pl.when(z >= s)
-            def _():
-                line = z - s
-                sbuf[a][line] = base(a, line).astype(sbuf[a].dtype)
-
-                @pl.when(z < lines - 1)
-                def _():
-                    along(a, line, False).wait_recv()
-                    sbuf[a][line] = (
-                        sbuf[a][line].astype(F32) + dbuf[a][line].astype(F32)
-                    ).astype(sbuf[a].dtype)
-
-                along(a, line, False).start()
-    for a in range(n):
-        pl.when(z > 0)(lambda: along(a, z, True).wait_recv())
-        pl.when(z < lines - 1)(lambda: along(a, z, False).wait_recv())
-        total = base(a, z)
-        total = total + jnp.where(z > 0, ubuf[a][z].astype(F32), 0.0)
-        total = total + jnp.where(z < lines - 1, dbuf[a][z].astype(F32), 0.0)
-        out[a][...] = total.astype(out[a].dtype)
-        for line in range(lines):
-            across(a, line).wait_send()
-            pl.when(z != line)(lambda: along(a, line, True).wait_send())
-
-
-def sum_rows(experts, *blocks):
-    n, lines = len(blocks), experts // 2
-    half = [pltpu.VMEM((lines,) + b.shape[1:], b.dtype) for b in blocks]
-    return pl.pallas_call(
-        functools.partial(scatter_kernel, lines),
-        out_shape=[jax.ShapeDtypeStruct(b.shape[1:], b.dtype) for b in blocks],
-        in_specs=[VM] * n,
-        out_specs=[VM] * n,
-        scratch_shapes=half * 4 + [pltpu.SemaphoreType.DMA((n, lines))] * 5,
-        compiler_params=pltpu.CompilerParams(
-            collective_id=1, has_side_effects=True, vmem_limit_bytes=40 << 20
-        ),
-    )(*blocks)
 
 
 def per_device(tokens, routes, gates, w_gate, w_up, w_down, cotangent):
@@ -417,43 +483,42 @@
     table = jnp.sum(jnp.where(chosen, gates[:, :, None], 0.0), axis=1)
     near = experts == 8
     if near:
-        hidden, gpg, upg, inner, xs, cs, pick, slot_gate = front(
+        inner, mixed, token_grad, w_gate_grad, w_up_grad, w_down_grad = layer(
             experts, slots, table.T, tokens, cotangent, wg, wu, wd
         )
-        slot_gate = slot_gate[:, 0]
-        inner = inner[:, :, :1].reshape(slots, 1)
-    else:
-        weight = lax.all_to_all(table.T, "expert", split_axis=0, concat_axis=0, tiled=True)
-        x = lax.all_gather(tokens, "expert", axis=0, tiled=True)
-        c = lax.all_gather(cotangent, "expert", axis=0, tiled=True)
-        weight = weight.reshape(experts * tok_rows)
-
-        routed = weight > 0.0
-        rank = jnp.cumsum(routed.astype(jnp.int32)) - 1
-        rank = jnp.where(routed, rank, -1)
-        place = jnp.arange(slots, dtype=jnp.int32)
-        place = (place // q ^ d) * q + place % q
-        hit = place[:, None] == rank[None, :]
-        pick = hit.astype(BF)
-        slot_gate = jnp.sum(jnp.where(hit, weight[None, :], 0.0), axis=1)
-
-        xs = dot(pick, x).astype(BF)
-        gate_pre = reduce_rows(dot(xs, wg).astype(BF))
-        up_pre = reduce_rows(dot(xs, wu).astype(BF))
-        cs = dot(pick, c).astype(BF)
-        raw_grad = reduce_rows(dot_nt(cs, wd).astype(BF))
-
-        own_gate = slot_gate[:q, None]
-        sig = jax.nn.sigmoid(gate_pre)
-        active = gate_pre * sig
-        hidden32 = active * up_pre
-        hidden = gather_rows(hidden32.astype(BF))
-        gate_inner = jnp.sum(hidden32 * raw_grad, axis=1)
-        hidden_grad = raw_grad * own_gate
-        gpg = gather_rows((hidden_grad * up_pre * sig * (1.0 + gate_pre * (1.0 - sig))).astype(BF))
-        upg = gather_rows((hidden_grad * active).astype(BF))
-
-        inner = gather_rows(gate_inner[:, None])
+        gate_grad = jnp.sum(jnp.where(chosen, inner.T[:, None, :], 0.0), axis=2)
+        return mixed, token_grad, gate_grad, w_gate_grad[None], w_up_grad[None], w_down_grad[None]
+    weight = lax.all_to_all(table.T, "expert", split_axis=0, concat_axis=0, tiled=True)
+    x = lax.all_gather(tokens, "expert", axis=0, tiled=True)
+    c = lax.all_gather(cotangent, "expert", axis=0, tiled=True)
+    weight = weight.reshape(experts * tok_rows)
+
+    routed = weight > 0.0
+    rank = jnp.cumsum(routed.astype(jnp.int32)) - 1
+    rank = jnp.where(routed, rank, -1)
+    place = jnp.arange(slots, dtype=jnp.int32)
+    place = (place // q ^ d) * q + place % q
+    hit = place[:, None] == rank[None, :]
+    pick = hit.astype(BF)
+    slot_gate = jnp.sum(jnp.where(hit, weight[None, :], 0.0), axis=1)
+
+    xs = dot(pick, x).astype(BF)
+    gate_pre = reduce_rows(dot(xs, wg).astype(BF))
+    up_pre = reduce_rows(dot(xs, wu).astype(BF))
+    cs = dot(pick, c).astype(BF)
+    raw_grad = reduce_rows(dot_nt(cs, wd).astype(BF))
+
+    own_gate = slot_gate[:q, None]
+    sig = jax.nn.sigmoid(gate_pre)
+    active = gate_pre * sig
+    hidden32 = active * up_pre
+    hidden = gather_rows(hidden32.astype(BF))
+    gate_inner = jnp.sum(hidden32 * raw_grad, axis=1)
+    hidden_grad = raw_grad * own_gate
+    gpg = gather_rows((hidden_grad * up_pre * sig * (1.0 + gate_pre * (1.0 - sig))).astype(BF))
+    upg = gather_rows((hidden_grad * active).astype(BF))
+
+    inner = gather_rows(gate_inner[:, None])
 
     out = (dot(hidden, wd) * slot_gate[:, None]).astype(BF)
     out = dot_t(pick, out).astype(BF)
@@ -461,18 +526,9 @@
     pair = dot_t(pick, pair).astype(BF)
 
     inner = jnp.sum(jnp.where(pick > 0, inner, 0.0), axis=0).reshape(experts, tok_rows)
-    if near:
-        mine = (labels == me)[None, :, None]
-        inner, mixed, token_grad = sum_rows(
-            experts,
-            jnp.where(mine, inner[:, None, :], 0.0),
-            out.reshape(experts, tok_rows, quarter),
-            pair.reshape(experts, tok_rows, quarter),
-        )
-    else:
-        inner = lax.all_to_all(inner, "expert", split_axis=0, concat_axis=0, tiled=True)
-        mixed = lax.psum_scatter(out, "expert", scatter_dimension=0, tiled=True)
-        token_grad = lax.psum_scatter(pair, "expert", scatter_dimension=0, tiled=True)
+    inner = lax.all_to_all(inner, "expert", split_axis=0, concat_axis=0, tiled=True)
+    mixed = lax.psum_scatter(out, "expert", scatter_dimension=0, tiled=True)
+    token_grad = lax.psum_scatter(pair, "expert", scatter_dimension=0, tiled=True)
     gate_grad = jnp.sum(jnp.where(chosen, inner.T[:, None, :], 0.0), axis=2)
 
     w_down_grad = dot_t((hidden.astype(F32) * slot_gate[:, None]).astype(BF), cs).astype(BF)[None]

time: 187 us -> 160 us (0.86)
  matrix products: 26.8 us -> 0 us
  local copies, waits for them, and re-layouts: 5.35 us -> 9.69 us
  Pallas kernels: 151 us -> 147 us
    dot_general x6 -> x0, matrix products: 26.8 us -> none  [the longest x5 21.9 us: dot_t(): lax.dot_general(a, b, (((0,), (0,)), ((), ())), preferred_element_type=F32)]
    unnamed x20 -> x11, local copies, waits for them, and re-layouts: 2.9 us -> 9.69 us
    pallas_call x2 -> x1, Pallas kernels: 151 us -> 147 us  [layer(): pl.pallas_call(functools.partial(layer_kernel, experts // 2), out_shape=[...]
    slice x2 -> x0, local copies, waits for them, and re-layouts: 2.37 us -> none  [the longest x1 1.2 us: per_device(): inner = inner[:, :, :1].reshape(slots, 1)]
where the time goes in v2:
time: 160 us
  Pallas kernels  147 us (92%)
  local copies, waits for them, and re-layouts  9.69 us (6%)
  other arithmetic  2.57 us (2%)
    pallas_call x1, Pallas kernels, layer(): pl.pallas_call(functools.partial(layer_kernel, experts // 2), out_shape=[...  147 us
    unnamed x11, local copies, waits for them, and re-layouts  9.69 us

profile of v2, /device:TPU:0, one launch (start us, length us, event | category | flops | bytes accessed | tf_op | source)
XLA Modules:
  0.0 160.0 jit_solution(4602114644679761048)
XLA Ops:
  0.6 1.3 select_reduce_fusion.1
  1.9 0.0 copy-start.2
  1.9 147.1 %shard_map.118 = (f32[8,128]{1,0:T(8,128)}, bf16[128,896]{1,0:T(8,128)(2,1)}, bf16[128,896]{1,0:T(8,128)(2,1)}, bf16[896,1024]{1,0:T(8,128)(2,1)}, bf16[896,1024]{1,0:T(8,128)(2,1)}, /*index=5*/bf16[1024,896]{1,0:T(8,128)(2,1)}) custom-call(f32[8,128]{1,0:T(8,128)} %bitcast.14, bf16[128,896]{1,0:T(8,128)(2,1)} %tok.1, bf16[128,896]{1,0:T(8,128)(2,1)} %cot.1, ...), custom_call_target="tpu_custom_call" | custom-call | tf_op jit(solution)/shard_map/pallas_call | solution.py:420
  149.1 0.0 copy-done.2
  149.1 1.3 select_reduce_fusion
  150.3 1.6 %copy.21 = bf16[128,896]{1,0:T(8,128)(2,1)} copy(bf16[128,896]{1,0:T(8,128)(2,1)} %get-tuple-element.24) | data formatting | bytes 458752
  152.0 1.6 %copy.22 = bf16[128,896]{1,0:T(8,128)(2,1)} copy(bf16[128,896]{1,0:T(8,128)(2,1)} %get-tuple-element.25) | data formatting | bytes 458752
  153.6 0.0 copy-start.1
  153.6 3.0 %copy.23 = bf16[1,896,1024]{2,1,0:T(8,128)(2,1)} copy(bf16[1,896,1024]{2,1,0:T(8,128)(2,1)} %bitcast.10) | data formatting | bytes 3670016
  156.6 0.0 copy-done.1
  156.6 0.0 copy-start
  156.6 1.2 copy.24
  157.9 0.9 copy-done
  158.8 1.2 copy.25
Async XLA Ops:
  1.9 147.1 %copy-start.2 = (s32[128,4]{0,1:T(4,128)S(1)}, s32[128,4]{0,1:T(4,128)}, u32[]{:S(2)}) copy-start(s32[128,4]{0,1:T(4,128)} %param.8) | copy-start | bytes 6148
  153.6 3.0 %copy-start.1 = (bf16[896,1024]{1,0:T(8,128)(2,1)S(1)}, bf16[896,1024]{1,0:T(8,128)(2,1)}, u32[]{:S(2)}) copy-start(bf16[896,1024]{1,0:T(8,128)(2,1)} %get-tuple-element.16) | copy-start | bytes 5505028
  156.6 2.2 %copy-start = (bf16[1024,896]{1,0:T(8,128)(2,1)S(1)}, bf16[1024,896]{1,0:T(8,128)(2,1)}, u32[]{:S(2)}) copy-start(bf16[1024,896]{1,0:T(8,128)(2,1)} %get-tuple-element.17) | copy-start | bytes 5505028
